TPU v7x, 512 devices: a whole 4x4x16 slice. The times are simulated.
512 devices in a mesh: paths: 8 (over y, core), tm: 64 (over z, x).
Axes of the slice: x: 4, y: 4, z: 16, core: 2. Of those that a mesh axis runs over, the one named last changes fastest.
Arguments:
- independent_disturbances: bfloat16 [4096, 32, 1024], P('tm', 'paths'), may hold values from -6 to 6
- starting_driver_values: float32 [32, 1024], P('paths'), may hold values from -6 to 6
- correlation_mixer: bfloat16 [1024, 1024], P('paths'), may hold values from -0.1875 to 0.1875
- log_persistence: float32 [1024], replicated, may hold values from -0.034 to 0
- regime_multiplier: float32 [4096], P('tm'), may hold values from 0.5 to 1
- payoff_per_unit_table: bfloat16 [1024, 128], replicated, may hold values from -0.1875 to 0.1875
- short_yield_coefficients: bfloat16 [1024], replicated, may hold values from -0.1875 to 0.1875
Outputs:
- values: float32 [32, 128], P('paths')
All inputs are finite; a program needn't handle non-finite values.
Results may differ from a plain program's by a relative error of at most 0.0004.
Values may be sent and summed in bfloat16 or wider, within the bound.
A program may use at most 64 MiB of HBM per device.

v0:
```python
import jax
import jax.numpy as jnp
from jax import lax
from jax.sharding import Mesh
from jax.sharding import PartitionSpec as P

TM = ("tm_0", "tm_1")


def filled_with(shard, identity):
    return jax.tree.map(
        lambda a, e: jnp.broadcast_to(jnp.asarray(e, a.dtype), a.shape), shard, identity
    )


def all_in_one(shard, axis):
    leaves = jax.tree.leaves(shard)
    sequence = sorted(range(len(leaves)), key=lambda k: -leaves[k].size)
    width = (1, *leaves[sequence[0]].shape)[-1]
    lines = [
        jnp.pad(leaves[k].reshape(-1), (0, -leaves[k].size % width)).reshape(-1, width)
        for k in sequence
    ]
    both, at, found = (lax.all_gather(jnp.concatenate(lines), axis), 0, {})
    for k, line in zip(sequence, lines):
        piece = both[:, at : at + len(line)].reshape(len(both), -1)
        found[k] = piece[:, : leaves[k].size].reshape(-1, *leaves[k].shape)
        at += len(line)
    numbers = iter(range(len(leaves)))
    return jax.tree.map(lambda _: found[next(numbers)], shard)


def carried_in(shard, axes, combine, identity):
    before = start = filled_with(shard, identity)
    running = shard
    for axis in reversed(axes):
        peers, here = (lax.axis_size(axis), lax.axis_index(axis))
        pieces = all_in_one(running, axis)
        inside, running = (start, start)
        for k in range(peers):
            passed = k < here
            running = combine(running, jax.tree.map(lambda part: part[k], pieces))
            inside = jax.tree.map(lambda new, old: jnp.where(passed, new, old), running, inside)
        before = combine(inside, before)
    return before


def copy_for_each(shard, axis):
    copies = jnp.broadcast_to(shard, (lax.axis_size(axis), *shard.shape))
    return lax.all_to_all(copies, axis, split_axis=0, concat_axis=0, tiled=True)


def combined_pairwise(pieces, combine):
    while len(jax.tree.leaves(pieces)[0]) > 1:
        pieces = jax.vmap(combine)(*(pieces[side::2] for side in (0, 1)))
    return pieces[0]


def prefix(shard, axis, combine, identity):
    peers, here = (lax.axis_size(axis), lax.axis_index(axis))
    passed = jnp.arange(peers) < here

    def kept(part, zero, own):
        part = jnp.where(
            passed.reshape(-1, *(1 for _ in own.shape)), part, jnp.asarray(zero, own.dtype)
        )
        return part

    pieces = copy_for_each(shard, axis)
    return combined_pairwise(kept(pieces, identity, shard), combine)


def of_everyone(shard, axis):
    return copy_for_each(shard, axis).sum(axis=0)


def local(
    independent_disturbances,
    starting_driver_values,
    correlation_mixer,
    log_persistence,
    regime_multiplier,
    payoff_per_unit_table,
    short_yield_coefficients,
):
    slab_days, group_paths, driver_value_history = independent_disturbances.shape
    where_now = lax.axis_index(TM)
    correlated_disturbances = jnp.einsum(
        "spf,fg->spg",
        independent_disturbances,
        lax.all_gather(correlation_mixer, "paths", axis=0, tiled=True),
        preferred_element_type=jnp.float32,
    )
    persistence_multiplier = jnp.exp(log_persistence)
    vol = jnp.sqrt(-jnp.expm1(2.0 * log_persistence))
    leading_element = jnp.where(
        where_now == 0, starting_driver_values, jnp.zeros_like(starting_driver_values)
    )

    def propagate_one_day(carry, operand_tensors):
        state, decay = carry
        random_normal_sample, regime_multiplier_today = operand_tensors
        driver_value_now = persistence_multiplier * regime_multiplier_today
        state = driver_value_now * state + vol * random_normal_sample
        decay = decay * driver_value_now
        return ((state, decay), (state, decay))

    (state, decay), (local_states, local_decays) = lax.scan(
        propagate_one_day,
        (leading_element, jnp.ones((driver_value_history,), jnp.float32)),
        (correlated_disturbances, regime_multiplier),
    )

    def chain(earlier, later):
        return (earlier[0] * later[0], later[0][None, :] * earlier[1] + later[1])

    identity = (
        jnp.ones((driver_value_history,), jnp.float32),
        jnp.zeros((group_paths, driver_value_history), jnp.float32),
    )
    carried = carried_in((decay, state), TM, chain, identity)
    driver_trajectory = local_states + local_decays[:, None, :] * carried[1][None, :, :]
    scenario = driver_trajectory.astype(jnp.bfloat16)
    horizon_days = slab_days * lax.axis_size(TM)
    cash = jnp.einsum(
        "tpf,fk->tpk", scenario, payoff_per_unit_table, preferred_element_type=jnp.float32
    )
    rate = 0.03 + 0.3 * jnp.einsum(
        "tpf,f->tp", scenario, short_yield_coefficients, preferred_element_type=jnp.float32
    )
    running = jnp.cumsum(rate, axis=0)

    def added(earlier, later):
        return earlier + later

    before = prefix(running[-1], TM, added, jnp.zeros((group_paths,), jnp.float32))
    discount = jnp.exp(-(1.0 / 256.0) * (before[None, :] + running))
    partial_sum = jnp.sum(discount[:, :, None] * cash, axis=0) / horizon_days
    return of_everyone(partial_sum, TM)


def solution(mesh):
    split = Mesh(mesh.devices.reshape(mesh.shape["paths"], 16, 4), ("paths", "tm_0", "tm_1"))
    placed = (P(TM, "paths", None), P("paths", None), P("paths", None), P(), P(TM), P(), P())
    return jax.shard_map(
        local, mesh=split, in_specs=placed, out_specs=P("paths", None), check_vma=False
    )
```

profile of v0, /device:TPU:2, one launch (start us, length us, event | category | flops | bytes accessed | tf_op | source)
XLA Modules:
  0.0 236.4 jit_solution(2021905275992335647)
XLA Ops:
  6.5 0.7 all-gather.6.cloned.1.call-update
  7.3 0.7 reshape.283
  8.0 0.7 negate_sqrt_fusion
  8.8 38.1 %all-gather.6.cloned.1.call-done = bf16[1024,1024]{1,0:T(8,128)(2,1)} async-done(((bf16[128,1024]{1,0:T(8,128)(2,1)}), bf16[1024,1024]{1,0:T(8,128)(2,1)}) %all-gather.6.cloned.1.call-update) | async-done | bytes 2097168 | tf_op jit(solution)/shard_map/all_gather | solution.py:91
  46.9 2.5 %fusion.2 = f32[64,4,1024]{2,0,1:T(8,128)S(1)} fusion(bf16[1024,1024]{1,0:T(8,128)(2,1)} %all-gather.6.cloned.1.call-done, bf16[64,4,1024]{2,1,0:T(4,128)(2,1)} %param.9), kind=kOutput, calls=%fused_computation.7 | convolution fusion | flops 536870912 | bytes 3670016 | tf_op jit(solution)/shard_map/spf,fg->spg/dot_general | solution.py:88
  49.4 85.9 %while.17 = (s32[]{:T(128)}, f32[4,1024]{1,0:T(4,128)S(1)}, f32[1024]{0:T(1024)S(1)}, f32[64,4,1024]{2,1,0:T(4,128)S(1)}, f32[64,1024]{1,0:T(8,128)S(1)}, /*inde...) while((s32[]{:T(128)}, f32[4,1024]{1,0:T(4,128)S(1)}, ...), condition=%wide.region_1.2_spmd.clone, body=%wide.region_0.1_spmd.clone.sunk | while | flops 15363 | bytes 131219 | solution.py:108
  49.4 0.6 dynamic_slice.14
  50.7 0.6 dynamic_slice.14
  52.1 0.6 dynamic_slice.14
  54.7 0.6 dynamic_slice.14
  57.4 0.6 dynamic_slice.14
  58.8 0.6 dynamic_slice.14
  60.1 0.6 dynamic_slice.14
  61.5 0.6 dynamic_slice.14
  64.1 0.6 dynamic_slice.14
  66.8 0.6 dynamic_slice.14
  68.2 0.6 dynamic_slice.14
  70.9 0.6 dynamic_slice.14
  73.5 0.6 dynamic_slice.14
  74.9 0.6 dynamic_slice.14
  76.2 0.6 dynamic_slice.14
  77.6 0.6 dynamic_slice.14
  80.3 0.6 dynamic_slice.14
  82.9 0.6 dynamic_slice.14
  84.3 0.6 dynamic_slice.14
  135.3 12.2 %all-gather.2 = f32[4,5,1024]{2,1,0:T(8,128)S(1)} all-gather(f32[1,5,1024]{2,1,0:T(8,128)S(1)} %maximum_bitcast_fusion), channel_id=2, replica_groups=mesh['paths'=8,'tm_0'=16,'tm_1'=4] {'tm_1'}, dimensions={0}, use_global_device_ids=true | all-gather | bytes 102400 | tf_op jit(solution)/shard_map/all_gather | solution.py:24
  147.6 33.2 %all-gather.3 = f32[16,5,1024]{2,1,0:T(8,128)S(1)} all-gather(f32[1,5,1024]{2,1,0:T(8,128)S(1)} %maximum_bitcast_fusion.1), channel_id=3, replica_groups=mesh['paths'=8,'tm_0'=16,'tm_1'=4] {'tm_0'}, dimensions={0}, use_global_device_ids=true | all-gather | bytes 348160 | tf_op jit(solution)/shard_map/all_gather | solution.py:24
  181.9 0.6 broadcast_in_dim.41
  182.5 11.7 %all-to-all-start = ((f32[64,1,4]{2,1,0:T(1,128)}), f32[64,1,4]{2,1,0:T(1,128)S(1)}, u32[]{:S(2)}, u32[]{:S(2)}) async-start(f32[64,1,4]{2,1,0:T(1,128)} %broadcast_in_dim.41), calls=%async_computation | async-start | bytes 65536 | tf_op jit(solution)/shard_map/all_to_all | solution.py:50
  194.3 13.8 %all-to-all-done = f32[64,1,4]{2,1,0:T(1,128)S(1)} async-done(((f32[64,1,4]{2,1,0:T(1,128)}), f32[64,1,4]{2,1,0:T(1,128)S(1)}, u32[]{:S(2)}, u32[]{:S(2)}) %all-to-all-start) | async-done | bytes 1056 | tf_op jit(solution)/shard_map/all_to_all | solution.py:50
  208.8 20.1 %all_to_all.14 = f32[64,4,128]{2,1,0:T(4,128)S(1)} all-to-all(f32[64,4,128]{2,1,0:T(4,128)S(1)} %broadcast_in_dim.43), channel_id=1, replica_groups=mesh['paths'=8,'tm_0'=16,'tm_1'=4] {'tm_0','tm_1'}, dimensions={0} | all-to-all | bytes 262144 | tf_op jit(solution)/shard_map/all_to_all | solution.py:50
  228.9 0.7 reduce_sum.19
  (346 shorter events, 74.1 us)
Async XLA Ops:
  6.5 201.9 %copy-start = (bf16[1024,128]{1,0:T(8,128)(2,1)S(1)}, bf16[1024,128]{1,0:T(8,128)(2,1)}, u32[]{:S(2)}) copy-start(bf16[1024,128]{1,0:T(8,128)(2,1)} %param.14) | copy-start | bytes 786436
  6.5 42.8 %copy-start.1 = (f32[64]{0:T(128)S(1)}, f32[64]{0:T(128)}, u32[]{:S(2)}) copy-start(f32[64]{0:T(128)} %param.13) | copy-start | bytes 772
  6.5 40.3 %all-gather.6.cloned.1.call-start = ((), (), s32[]{:S(2)}) async-start(), calls=%async_computation.2 | async-start | bytes 2359296 | tf_op jit(solution)/shard_map/all_gather | solution.py:91
  182.5 25.5 %all-to-all-start = ((f32[64,1,4]{2,1,0:T(1,128)}), f32[64,1,4]{2,1,0:T(1,128)S(1)}, u32[]{:S(2)}, u32[]{:S(2)}) async-start(f32[64,1,4]{2,1,0:T(1,128)} %broadcast_in_dim.41), calls=%async_computation | async-start | bytes 65536 | tf_op jit(solution)/shard_map/all_to_all | solution.py:50
Sparse Core Ops, SparseCore 0:
  9.5 37.2 all-gather.5
where the time goes:
time: 237 us; the launch traced here: 236 us
  blocking collectives  65.5 us (28%)
  waiting for transfers between devices  52.6 us (22%)
  local copies, waits for them, and re-layouts  47.2 us (20%)
  other arithmetic  39.9 us (17%)
  between operations  13.6 us (6%)
  starting transfers between devices  11.7 us (5%)
  matrix products  3.15 us (1%)
  loops' own time  2.69 us (1%)
    all_gather x2, blocking collectives, all_in_one(): both, at, found = (lax.all_gather(jnp.concatenate(lines), axis), 0, {})  45.4 us
    dynamic_slice x128, local copies, waits for them, and re-layouts, local(): lax.scan(propagate_one_day, (leading_element, jnp.ones((driver_value_hist...  38.5 us
    all_gather x1, waiting for transfers between devices, local(): lax.all_gather(correlation_mixer, 'paths', axis=0, tiled=True)  38.1 us
    mul x64, other arithmetic, propagate_one_day(): decay = decay * driver_value_now  36 us
    all_to_all x1, blocking collectives, copy_for_each(): return lax.all_to_all(copies, axis, split_axis=0, concat_axis=0, tiled=True)  20.1 us
    all_to_all x1, waiting for transfers between devices, copy_for_each(): return lax.all_to_all(copies, axis, split_axis=0, concat_axis=0, tiled=True)  13.8 us
    all_to_all x1, starting transfers between devices, copy_for_each(): return lax.all_to_all(copies, axis, split_axis=0, concat_axis=0, tiled=True)  11.7 us
    dynamic_update_slice x64, local copies, waits for them, and re-layouts, local(): lax.scan(propagate_one_day, (leading_element, jnp.ones((driver_value_hist...  7.04 us
  transfers between devices with their start and end apart: 2, of which 2 were waited for; matrix products, arithmetic and copies ran while one was open for 1% of the time, Pallas kernels for 0%

commit v1 on v0

--- a/solution.py
+++ b/solution.py
@@ -88,7 +88,10 @@
     correlated_disturbances = jnp.einsum(
         "spf,fg->spg",
         independent_disturbances,
-        lax.all_gather(correlation_mixer, "paths", axis=0, tiled=True),
+        jnp.concatenate(
+            lax.all_to_all(jnp.stack([correlation_mixer] * lax.axis_size("paths")), "paths", 0, 0),
+            axis=0,
+        ),
         preferred_element_type=jnp.float32,
     )
     persistence_multiplier = jnp.exp(log_persistence)

time: 237 us -> 356 us (1.50); the launches traced: 236 us -> 351 us
  local copies, waits for them, and re-layouts: 47.2 us -> 135 us
  other arithmetic: 39.9 us -> 85.8 us
  between operations: 13.6 us -> 0.25 us
  waiting for transfers between devices: 52.6 us -> 40.6 us
  blocking collectives: 65.5 us -> 70.8 us
    dynamic_update_slice x64, local copies, waits for them, and re-layouts: 7.04 us -> 88.5 us  [local(): lax.scan(propagate_one_day, (leading_element, jnp.ones((driver_value_hist...]
    all_gather x1 -> x0, waiting for transfers between devices: 38.1 us -> none  [local(): lax.all_gather(correlation_mixer, 'paths', axis=0, tiled=True)]
    dynamic_update_slice x64, other arithmetic: 1.72 us -> 39.6 us  [local(): lax.scan(propagate_one_day, (leading_element, jnp.ones((driver_value_hist...]
    all_to_all x0 -> x1, waiting for transfers between devices: none -> 27 us  [local(): lax.all_to_all(jnp.stack([correlation_mixer] * lax.axis_size('paths')), '...]
    mul x64, other arithmetic: 36 us -> 43.8 us  [propagate_one_day(): decay = decay * driver_value_now]
    all_gather x2, blocking collectives: 45.4 us -> 50.5 us  [all_in_one(): both, at, found = (lax.all_gather(jnp.concatenate(lines), axis), 0, {})]
    all_to_all x0 -> x1, starting transfers between devices: none -> 4.6 us  [local(): lax.all_to_all(jnp.stack([correlation_mixer] * lax.axis_size('paths')), '...]
    dynamic_slice x128, local copies, waits for them, and re-layouts: 38.5 us -> 43.1 us  [local(): lax.scan(propagate_one_day, (leading_element, jnp.ones((driver_value_hist...]
  transfers between devices with their start and end apart: 2 -> 2, of which waited for: 2 -> 2; matrix products, arithmetic and copies ran while one was open for 1% -> 0% of each run, Pallas kernels for 0% -> 0%
where the time goes in v1:
time: 356 us; the launch traced here: 351 us
  local copies, waits for them, and re-layouts  135 us (38%)
  other arithmetic  85.8 us (24%)
  blocking collectives  70.8 us (20%)
  waiting for transfers between devices  40.6 us (11%)
  starting transfers between devices  14.4 us (4%)
    dynamic_update_slice x64, local copies, waits for them, and re-layouts, local(): lax.scan(propagate_one_day, (leading_element, jnp.ones((driver_value_hist...  88.5 us
    all_gather x2, blocking collectives, all_in_one(): both, at, found = (lax.all_gather(jnp.concatenate(lines), axis), 0, {})  50.5 us
    mul x64, other arithmetic, propagate_one_day(): decay = decay * driver_value_now  43.8 us
    dynamic_slice x128, local copies, waits for them, and re-layouts, local(): lax.scan(propagate_one_day, (leading_element, jnp.ones((driver_value_hist...  43.1 us
    dynamic_update_slice x64, other arithmetic, local(): lax.scan(propagate_one_day, (leading_element, jnp.ones((driver_value_hist...  39.6 us
    all_to_all x1, waiting for transfers between devices, local(): lax.all_to_all(jnp.stack([correlation_mixer] * lax.axis_size('paths')), '...  27 us
    all_to_all x1, blocking collectives, copy_for_each(): return lax.all_to_all(copies, axis, split_axis=0, concat_axis=0, tiled=True)  20.3 us
    all_to_all x1, waiting for transfers between devices, copy_for_each(): return lax.all_to_all(copies, axis, split_axis=0, concat_axis=0, tiled=True)  13.6 us
  transfers between devices with their start and end apart: 2, of which 2 were waited for; matrix products, arithmetic and copies ran while one was open for 0% of the time, Pallas kernels for 0%

profile of v1, /device:TPU:2, one launch (start us, length us, event | category | flops | bytes accessed | tf_op | source)
XLA Modules:
  0.0 350.7 jit_solution(5470583980798373335)
XLA Ops:
  0.0 2.6 stack.2
  2.6 4.6 %all-to-all-start = ((bf16[8,128,1024]{2,1,0:T(8,128)(2,1)}), bf16[8,128,1024]{2,1,0:T(8,128)(2,1)S(1)}, u32[]{:S(2)}, u32[]{:S(2)}) async-start(bf16[8,128,1024]{2,1,0:T(8,128)(2,1)} %stack.2), calls=%async_computation | async-start | bytes 4194304 | tf_op jit(solution)/shard_map/all_to_all | solution.py:92
  7.4 27.0 %all-to-all-done = bf16[8,128,1024]{2,1,0:T(8,128)(2,1)S(1)} async-done(((bf16[8,128,1024]{2,1,0:T(8,128)(2,1)}), bf16[8,128,1024]{2,1,0:T(8,128)(2,1)S(1)}, u32[]{:S(2)}, u32[]{:S(2)}) %all-to-all-start) | async-done | bytes 2097184 | tf_op jit(solution)/shard_map/all_to_all | solution.py:92
  34.4 1.8 fusion.3
  36.2 216.0 %while.17 = (s32[]{:T(128)}, f32[4,1024]{1,0:T(4,128)S(1)}, f32[1024]{0:T(1024)S(1)}, f32[64,4,1024]{2,1,0:T(4,128)}, f32[64,1024]{1,0:T(8,128)}, /*index=5*/f32...) while((s32[]{:T(128)}, f32[4,1024]{1,0:T(4,128)S(1)}, ...), condition=%wide.region_1.2_spmd.clone, body=%wide.region_0.1_spmd.clone.sunk | while | flops 15363 | bytes 131727 | solution.py:111
  38.2 1.4 dynamic_update_slice.14
  41.6 1.4 dynamic_update_slice.14
  45.0 1.4 dynamic_update_slice.14
  48.4 1.4 dynamic_update_slice.14
  51.8 1.4 dynamic_update_slice.14
  55.2 1.4 dynamic_update_slice.14
  58.5 1.4 dynamic_update_slice.14
  61.9 1.4 dynamic_update_slice.14
  65.3 1.4 dynamic_update_slice.14
  68.7 1.4 dynamic_update_slice.14
  72.1 1.4 dynamic_update_slice.14
  75.4 1.4 dynamic_update_slice.14
  78.8 1.4 dynamic_update_slice.14
  82.2 1.4 dynamic_update_slice.14
  200.3 1.4 dynamic_update_slice.14
  203.6 1.4 dynamic_update_slice.14
  207.0 1.4 dynamic_update_slice.14
  210.4 1.4 dynamic_update_slice.14
  213.8 1.4 dynamic_update_slice.14
  217.2 1.4 dynamic_update_slice.14
  220.5 1.4 dynamic_update_slice.14
  223.9 1.4 dynamic_update_slice.14
  252.3 13.9 %all-gather.2 = f32[4,5,1024]{2,1,0:T(8,128)S(1)} all-gather(f32[1,5,1024]{2,1,0:T(8,128)S(1)} %maximum_bitcast_fusion), channel_id=2, replica_groups=mesh['paths'=8,'tm_0'=16,'tm_1'=4] {'tm_1'}, dimensions={0}, use_global_device_ids=true | all-gather | bytes 102400 | tf_op jit(solution)/shard_map/all_gather | solution.py:24
  266.2 36.7 %all-gather.3 = f32[16,5,1024]{2,1,0:T(8,128)S(1)} all-gather(f32[1,5,1024]{2,1,0:T(8,128)S(1)} %maximum_bitcast_fusion.1), channel_id=3, replica_groups=mesh['paths'=8,'tm_0'=16,'tm_1'=4] {'tm_0'}, dimensions={0}, use_global_device_ids=true | all-gather | bytes 348160 | tf_op jit(solution)/shard_map/all_gather | solution.py:24
  305.6 9.8 %all-to-all-start.1 = ((f32[64,1,4]{2,1,0:T(1,128)}), f32[64,1,4]{2,1,0:T(1,128)S(1)}, u32[]{:S(2)}, u32[]{:S(2)}) async-start(f32[64,1,4]{2,1,0:T(1,128)} %broadcast_in_dim.41), calls=%async_computation.1 | async-start | bytes 65536 | tf_op jit(solution)/shard_map/all_to_all | solution.py:50
  315.4 13.6 %all-to-all-done.1 = f32[64,1,4]{2,1,0:T(1,128)S(1)} async-done(((f32[64,1,4]{2,1,0:T(1,128)}), f32[64,1,4]{2,1,0:T(1,128)S(1)}, u32[]{:S(2)}, u32[]{:S(2)}) %all-to-all-start.1) | async-done | bytes 1056 | tf_op jit(solution)/shard_map/all_to_all | solution.py:50
  329.8 20.3 %all_to_all.19 = f32[64,4,128]{2,1,0:T(4,128)S(1)} all-to-all(f32[64,4,128]{2,1,0:T(4,128)S(1)} %broadcast_in_dim.43), channel_id=1, replica_groups=mesh['paths'=8,'tm_0'=16,'tm_1'=4] {'tm_0','tm_1'}, dimensions={0} | all-to-all | bytes 262144 | tf_op jit(solution)/shard_map/all_to_all | solution.py:50
  (354 shorter events, 188.6 us)
Async XLA Ops:
  0.0 329.4 %copy-start = (bf16[1024,128]{1,0:T(8,128)(2,1)S(1)}, bf16[1024,128]{1,0:T(8,128)(2,1)}, u32[]{:S(2)}) copy-start(bf16[1024,128]{1,0:T(8,128)(2,1)} %param.14) | copy-start | bytes 786436
  2.6 4.7 %copy-start.4 = (bf16[1024]{0:T(1024)(128)(2,1)S(1)}, bf16[1024]{0:T(1024)(128)(2,1)}, u32[]{:S(2)}) copy-start(bf16[1024]{0:T(1024)(128)(2,1)} %param.15) | copy-start | bytes 6148
  2.6 4.7 %copy-start.3 = (f32[1024]{0:T(1024)S(1)}, f32[1024]{0:T(1024)}, u32[]{:S(2)}) copy-start(f32[1024]{0:T(1024)} %param.12) | copy-start | bytes 12292
  2.6 4.7 %copy-start.2 = (f32[4,1024]{1,0:T(4,128)S(1)}, f32[4,1024]{1,0:T(4,128)}, u32[]{:S(2)}) copy-start(f32[4,1024]{1,0:T(4,128)} %param.10) | copy-start | bytes 49156
  2.6 31.8 %all-to-all-start = ((bf16[8,128,1024]{2,1,0:T(8,128)(2,1)}), bf16[8,128,1024]{2,1,0:T(8,128)(2,1)S(1)}, u32[]{:S(2)}, u32[]{:S(2)}) async-start(bf16[8,128,1024]{2,1,0:T(8,128)(2,1)} %stack.2), calls=%async_computation | async-start | bytes 4194304 | tf_op jit(solution)/shard_map/all_to_all | solution.py:92
  7.2 29.0 %copy-start.5 = (f32[64]{0:T(128)S(1)}, f32[64]{0:T(128)}, u32[]{:S(2)}) copy-start(f32[64]{0:T(128)} %param.13) | copy-start | bytes 772
  252.3 50.9 %copy-start.1 = (f32[64,4,1024]{2,1,0:T(4,128)S(1)}, f32[64,4,1024]{2,1,0:T(4,128)}, u32[]{:S(2)}) copy-start(f32[64,4,1024]{2,1,0:T(4,128)} %get-tuple-element.55) | copy-start | bytes 3145732
  305.6 23.4 %all-to-all-start.1 = ((f32[64,1,4]{2,1,0:T(1,128)}), f32[64,1,4]{2,1,0:T(1,128)S(1)}, u32[]{:S(2)}, u32[]{:S(2)}) async-start(f32[64,1,4]{2,1,0:T(1,128)} %broadcast_in_dim.41), calls=%async_computation.1 | async-start | bytes 65536 | tf_op jit(solution)/shard_map/all_to_all | solution.py:50
